TPU v7x, 32 devices: a whole 2x2x4 slice. The times are simulated.
32 devices in a mesh: ctx: 8 (over z, x), head: 4 (over y, core).
Axes of the slice: x: 2, y: 2, z: 4, core: 2. Of those that a mesh axis runs over, the one named last changes fastest.
Arguments:
- queries: bfloat16 [1024, 4096], P('ctx', 'head'), may hold values from -5 to 5
- keys: bfloat16 [1024, 4096], P('ctx', 'head'), may hold values from -5 to 5
- values: bfloat16 [1024, 4096], P('ctx', 'head'), may hold values from -6 to 6
- episode: int32 [1024], P('ctx'), may hold values from 0 to 30, as said below
- out_weight: bfloat16 [4096, 4096], P('head'), may hold values from -1.5 to 1.5
- d_out: bfloat16 [1024, 4096], P(('ctx', 'head')), may hold values from -0.3984375 to 0.3984375
Outputs:
- mixed: bfloat16 [1024, 4096], P(('ctx', 'head'))
- d_queries: bfloat16 [1024, 4096], P('ctx', 'head')
- d_keys: bfloat16 [1024, 4096], P('ctx', 'head')
- d_values: bfloat16 [1024, 4096], P('ctx', 'head')
Inputs may be any that keep to these rules, and one draw needn't show every extreme that they name: Episode numbers never fall as time rises; the episode of time step t is 0 for t < 64 and 2 * (t // 64) - 1 or 2 * (t // 64) otherwise (so each episode has 1 to 64 time steps, and episode 0 has exactly 64).
All inputs are finite; a program needn't handle non-finite values.
Results may differ from a plain program's by a relative error of at most 0.02.
Values may be sent and summed in bfloat16 or wider, within the bound.
A program may use at most 64 MiB of HBM per device.

v0:
```python
import jax
import jax.numpy as jnp
from jax import lax
from jax.sharding import PartitionSpec as P

HD = 128


floor_score = -1e30


def time_steps(rows, rows_local, ctx_count):
    half_rows = rows_local // 2
    holder = rows // rows_local
    offset = rows % rows_local
    return jnp.where(
        offset < half_rows,
        holder * half_rows + offset,
        (2 * ctx_count - 1 - holder) * half_rows + offset - half_rows,
    )


def on_device(queries, keys, values, episode, out_weight, d_out):
    rows_local = queries.shape[0]
    width = queries.shape[1]
    heads = width // HD
    scale = HD ** (-0.5)
    place = lax.axis_index("ctx")
    ctx_count = lax.axis_size("ctx")
    window = 2 * ctx_count
    d_attn = lax.dot_general(
        lax.all_gather(d_out, "head", axis=0, tiled=True),
        out_weight,
        (((1,), (1,)), ((), ())),
        preferred_element_type=jnp.float32,
    ).astype(jnp.bfloat16)
    keys_all, values_all, episode_all = (
        lax.all_gather(keys, "ctx", axis=0, tiled=True),
        lax.all_gather(values, "ctx", axis=0, tiled=True),
        lax.all_gather(episode, "ctx", axis=0, tiled=True),
    )
    total = keys_all.shape[0]
    query_pos = place * rows_local + jnp.arange(rows_local, dtype=jnp.int32)
    query_time = time_steps(query_pos, rows_local, ctx_count)
    key_time = time_steps(jnp.arange(total, dtype=jnp.int32), rows_local, ctx_count)
    visible = (key_time[None, :] <= query_time[:, None]) & (
        episode[:, None] - episode_all[None, :] < window
    )
    query_heads = queries.reshape(rows_local, heads, HD)
    key_heads = keys_all.reshape(total, heads, HD)
    value_heads = values_all.reshape(total, heads, HD)
    scores = (
        jnp.einsum("qhd,khd->hqk", query_heads, key_heads, preferred_element_type=jnp.float32)
        * scale
    )
    scores = jnp.where(visible[None], scores, floor_score)
    top = jnp.max(scores, axis=2)
    lse = top + jnp.log(jnp.sum(jnp.exp(scores - top[:, :, None]), axis=2))
    probs = jnp.exp(scores - lse[:, :, None])
    probs_low = probs.astype(jnp.bfloat16)
    attn_heads = jnp.einsum(
        "hqk,khd->qhd", probs_low, value_heads, preferred_element_type=jnp.float32
    ).astype(jnp.bfloat16)
    attn = attn_heads.reshape(rows_local, width)
    mixed = lax.psum_scatter(
        jnp.dot(attn, out_weight, preferred_element_type=jnp.float32),
        "head",
        scatter_dimension=0,
        tiled=True,
    ).astype(jnp.bfloat16)
    d_heads = d_attn.reshape(rows_local, heads, HD)
    delta = jnp.sum(d_heads.astype(jnp.float32) * attn_heads.astype(jnp.float32), axis=2).T
    d_probs = jnp.einsum("qhd,khd->hqk", d_heads, value_heads, preferred_element_type=jnp.float32)
    d_scores = (probs * (d_probs - delta[:, :, None])).astype(jnp.bfloat16)
    dq_sum = jnp.einsum("hqk,khd->qhd", d_scores, key_heads, preferred_element_type=jnp.float32)
    d_queries = (scale * dq_sum).astype(jnp.bfloat16).reshape(rows_local, width)
    lse_all, delta_all = (
        lax.all_gather(lse.T, "ctx", axis=0, tiled=True),
        lax.all_gather(delta.T, "ctx", axis=0, tiled=True),
    )
    own_keys = keys.reshape(rows_local, heads, HD)
    own_values = values.reshape(rows_local, heads, HD)
    piece_q = lax.all_gather(queries, "ctx", axis=0, tiled=True)
    piece_d = lax.all_gather(d_attn, "ctx", axis=0, tiled=True)
    piece_ep = lax.all_gather(episode, "ctx", axis=0, tiled=True)
    count = piece_q.shape[0]
    piece_qh = piece_q.reshape(count, heads, HD)
    piece_dh = piece_d.reshape(count, heads, HD)
    piece_pos = jnp.arange(count, dtype=jnp.int32)
    piece_time = time_steps(piece_pos, rows_local, ctx_count)
    piece_mask = (query_time[None, :] <= piece_time[:, None]) & (
        piece_ep[:, None] - episode[None, :] < window
    )
    piece_scores = (
        jnp.einsum("qhd,khd->hqk", piece_qh, own_keys, preferred_element_type=jnp.float32) * scale
    )
    piece_scores = jnp.where(piece_mask[None], piece_scores, floor_score)
    piece_lse = lse_all.T
    piece_delta = delta_all.T
    piece_probs = jnp.exp(piece_scores - piece_lse[:, :, None])
    piece_dprobs = jnp.einsum(
        "qhd,khd->hqk", piece_dh, own_values, preferred_element_type=jnp.float32
    )
    piece_ds = (piece_probs * (piece_dprobs - piece_delta[:, :, None])).astype(jnp.bfloat16)
    dk_sum = jnp.einsum("hqk,qhd->khd", piece_ds, piece_qh, preferred_element_type=jnp.float32)
    dv_sum = jnp.einsum(
        "hqk,qhd->khd",
        piece_probs.astype(jnp.bfloat16),
        piece_dh,
        preferred_element_type=jnp.float32,
    )
    d_keys = (scale * dk_sum).astype(jnp.bfloat16).reshape(rows_local, width)
    d_values = dv_sum.astype(jnp.bfloat16).reshape(rows_local, width)
    return (mixed, d_queries, d_keys, d_values)


def solution(mesh):
    placed = (
        P("ctx", "head"),
        P("ctx", "head"),
        P("ctx", "head"),
        P("ctx"),
        P("head", None),
        P(("ctx", "head"), None),
    )
    return jax.shard_map(
        on_device,
        mesh=mesh,
        in_specs=placed,
        out_specs=(P(("ctx", "head"), None), P("ctx", "head"), P("ctx", "head"), P("ctx", "head")),
        check_vma=False,
    )
```

profile of v0, /device:TPU:0, one launch (start us, length us, event | category | flops | bytes accessed | tf_op | source)
XLA Modules:
  0.0 275.9 jit_solution(8874532666696596937)
XLA Ops:
  8.7 1.8 copy.32
  10.6 1.8 copy.39
  12.4 16.6 %all-gather.11.cloned.1.call-done = bf16[128,4096]{1,0:T(8,128)(2,1)} async-done(((bf16[32,4096]{1,0:T(8,128)(2,1)}), bf16[128,4096]{1,0:T(8,128)(2,1)}) %all-gather.11.cloned.1.call-update) | async-done | bytes 1048592 | tf_op jit(solution)/shard_map/all_gather | solution.py:32
  29.0 7.3 %convolution_convert_fusion = bf16[128,1024]{1,0:T(8,128)(2,1)} fusion(bf16[128,4096]{1,0:T(8,128)(2,1)} %all-gather.11.cloned.1.call-done, bf16[1024,4096]{1,0:T(8,128)(2,1)} %param.10), kind=kOutput, calls=%fused_computation.27 | convolution fusion | flops 1073872896 | bytes 9699328 | tf_op jit(solution)/shard_map/dot_general | solution.py:31
  36.4 20.4 %all-gather = s32[8,1,128]{2,1,0:T(1,128)S(1)} all-gather(s32[1,1,128]{2,1,0:T(1,128)S(1)} %bitcast.84), channel_id=1, replica_groups=mesh['ctx'=8,'head'=4] {'ctx'}, dimensions={0}, use_global_device_ids=true | all-gather | bytes 4608 | tf_op jit(solution)/shard_map/all_gather | solution.py:40
  57.1 1.2 copy.36
  58.3 22.2 %all-gather.9.cloned.1.call-done = bf16[1024,1024]{1,0:T(8,128)(2,1)} async-done(((bf16[128,1024]{1,0:T(8,128)(2,1)}), bf16[1024,1024]{1,0:T(8,128)(2,1)}) %all-gather.9.cloned.1.call-update) | async-done | bytes 2097168 | tf_op jit(solution)/shard_map/all_gather | solution.py:39
  80.5 2.9 %copy.35 = bf16[1024,1024]{0,1:T(8,128)(2,1)S(1)} copy(bf16[1024,1024]{1,0:T(8,128)(2,1)} %all-gather.9.cloned.1.call-done) | data formatting | bytes 4194304 | tf_op jit(solution)/shard_map/all_gather | solution.py:39
  83.4 49.3 %all-gather.7.cloned.1.call-done = bf16[1024,1024]{0,1:T(8,128)(2,1)} async-done(((bf16[128,1024]{0,1:T(8,128)(2,1)}), bf16[1024,1024]{0,1:T(8,128)(2,1)}) %all-gather.7.cloned.1.call-update) | async-done | bytes 2097168 | tf_op jit(solution)/shard_map/all_gather | solution.py:38
  132.7 2.8 %fusion.2 = (f32[8,128]{1,0:T(8,128)S(1)}, f32[8,128,1024]{2,1,0:T(8,128)S(1)}) fusion(pred[128,1024]{1,0:T(8,128)(4,1)S(1)} %fusion.27, bf16[1024,8,128]{0,2,1:T(8,128)(2,1)} %bitcast.67, bf16[128,1024]{1,0:T(8,128)(2,1)S(1)} %copy-done.4), kind=kOutput, calls=%fused_computation.8 | convolution fusion | flops 271580160 | bytes 6688768 | tf_op jit(solution)/shard_map/qhd,khd->hqk/dot_general | solution.py:53
  135.6 1.1 exponential_reduce_fusion
  136.7 1.4 multiply_reduce_fusion
  138.1 1.2 slice-done.1
  139.3 2.7 fusion.62
  142.3 5.1 %fusion.19 = bf16[8,128,128]{1,2,0:T(8,128)(2,1)S(1)} fusion(bf16[1024,8,128]{0,2,1:T(8,128)(2,1)S(1)} %bitcast.68, f32[8,128,1024]{2,1,0:T(8,128)} %copy-done, bf16[128,8,128]{0,2,1:T(8,128)(2,1)S(1)} %bitcast.74, bf16[1024,8,128]{0,2,1:T(8,128)(2,1)} %bitcast.70, f32[8,128]{1,0:T(8,128)S(1)} %bitcast.85, f32[8,128]{1,0:T(8,128)S(1)} %log_add_fusion, ...), kind=kOutput, calls=%fused_computation.23 | convolution fusion | flops 543424512 | bytes 9052160 | tf_op jit(solution)/shard_map/hqk,khd->qhd/dot_general | solution.py:75
  148.2 30.6 %all_gather.32 = f32[1024,8]{0,1:T(8,128)S(1)} all-gather(f32[128,8]{0,1:T(8,128)S(1)} %get-tuple-element.18), channel_id=1, replica_groups=mesh['ctx'=8,'head'=4] {'ctx'}, dimensions={0}, use_global_device_ids=true | all-gather | bytes 36864 | tf_op jit(solution)/shard_map/all_gather | solution.py:79
  178.8 30.9 %all_gather.30 = f32[1024,8]{0,1:T(8,128)S(1)} all-gather(f32[128,8]{0,1:T(8,128)S(1)} %bitcast.83), channel_id=1, replica_groups=mesh['ctx'=8,'head'=4] {'ctx'}, dimensions={0}, use_global_device_ids=true | all-gather | bytes 36864 | tf_op jit(solution)/shard_map/all_gather | solution.py:78
  209.8 4.5 %fusion.33 = f32[8,1024,128]{2,1,0:T(8,128)} fusion(bf16[1024,8,128]{0,2,1:T(8,128)(2,1)} %bitcast.65, bf16[128,1024]{1,0:T(8,128)(2,1)S(1)} %copy-done.5), kind=kOutput, calls=%fused_computation.35 | convolution fusion | flops 268435456 | bytes 6553600 | tf_op jit(solution)/shard_map/qhd,khd->hqk/dot_general | solution.py:95
  214.2 20.7 %all-gather.15.cloned.1.call-done = bf16[1024,1024]{1,0:T(8,128)(2,1)} async-done(((bf16[128,1024]{1,0:T(8,128)(2,1)}), bf16[1024,1024]{1,0:T(8,128)(2,1)}) %all-gather.15.cloned.1.call-update) | async-done | bytes 2097168 | tf_op jit(solution)/shard_map/all_gather | solution.py:84
  234.9 4.0 %copy.52 = bf16[1024,1024]{0,1:T(8,128)(2,1)} copy(bf16[1024,1024]{1,0:T(8,128)(2,1)} %all-gather.15.cloned.1.call-done) | data formatting | bytes 4194304 | tf_op jit(solution)/shard_map/reshape | solution.py:88
  238.9 6.2 %fusion.20 = bf16[8,128,128]{1,2,0:T(8,128)(2,1)S(1)} fusion(bf16[1024,8,128]{0,2,1:T(8,128)(2,1)S(1)} %bitcast.66, f32[8,1024,128]{2,1,0:T(8,128)} %fusion.33, bf16[1024,8,128]{0,2,1:T(8,128)(2,1)} %bitcast.71, f32[8,1024]{1,0:T(8,128)S(1)} %bitcast.82, f32[8,1024]{1,0:T(8,128)S(1)} %bitcast.80, pred[1024,128]{1,0:T(8,128)(4,1)S(1)} %fusion.28, ...), kind=kOutput, calls=%fused_computation.24 | convolution fusion | flops 543424512 | bytes 9109504 | tf_op jit(solution)/shard_map/hqk,qhd->khd/dot_general | solution.py:105
  245.9 3.7 %fusion.24 = bf16[8,128,128]{2,1,0:T(8,128)(2,1)S(1)} fusion(bf16[1024,8,128]{0,2,1:T(8,128)(2,1)} %bitcast.72, f32[8,1024,128]{2,1,0:T(8,128)} %fusion.33, f32[8,1024]{1,0:T(8,128)S(1)} %bitcast.81, pred[1024,128]{1,0:T(8,128)(4,1)S(1)} %fusion.28), kind=kOutput, calls=%fused_computation.26 | convolution fusion | flops 272760832 | bytes 6717440 | tf_op jit(solution)/shard_map/hqk,qhd->khd/dot_general | solution.py:106
  250.5 16.7 %reduce-scatter.2.cloned.1.call-done = f32[32,4096]{1,0:T(8,128)} async-done(((f32[128,4096]{1,0:T(8,128)}), f32[32,4096]{1,0:T(8,128)}) %reduce-scatter.2.cloned.1.call-update) | async-done | bytes 524304 | tf_op jit(solution)/shard_map/reduce_scatter | solution.py:65
  267.3 1.8 convert_element_type.51
  (41 shorter events, 4.8 us)
Async XLA Ops:
  7.2 21.9 %all-gather.11.cloned.1.call-start = ((), (), s32[]{:S(2)}) async-start(), calls=%async_computation.4 | async-start | bytes 1310720 | tf_op jit(solution)/shard_map/all_gather | solution.py:32
  7.9 72.6 %all-gather.9.cloned.1.call-start = ((), (), s32[]{:S(2)}) async-start(), calls=%async_computation.2 | async-start | bytes 2359296 | tf_op jit(solution)/shard_map/all_gather | solution.py:39
  8.6 124.1 %all-gather.7.cloned.1.call-start = ((), (), s32[]{:S(2)}) async-start(), calls=%async_computation.1 | async-start | bytes 2359296 | tf_op jit(solution)/shard_map/all_gather | solution.py:38
  10.5 199.2 %all-gather.13.cloned.1.call-start = ((), (), s32[]{:S(2)}) async-start(), calls=%async_computation.5 | async-start | bytes 2359296 | tf_op jit(solution)/shard_map/all_gather | solution.py:83
  12.4 24.1 %copy-start.7 = (s32[128]{0:T(128)S(1)}, s32[128]{0:T(128)}, u32[]{:S(2)}) copy-start(s32[128]{0:T(128)} %param.9) | copy-start | bytes 1540
  12.4 222.5 %all-gather.15.cloned.1.call-start = ((), (), s32[]{:S(2)}) async-start(), calls=%async_computation.6 | async-start | bytes 2359296 | tf_op jit(solution)/shard_map/all_gather | solution.py:84
  36.3 96.4 %copy-start.4 = (bf16[128,1024]{1,0:T(8,128)(2,1)S(1)}, bf16[128,1024]{1,0:T(8,128)(2,1)}, u32[]{:S(2)}) copy-start(bf16[128,1024]{1,0:T(8,128)(2,1)} %param.6) | copy-start | bytes 786436
  36.4 230.9 %reduce-scatter.2.cloned.1.call-start = ((), (), s32[]{:S(2)}) async-start(), calls=%async_computation.3 | async-start | bytes 2621440 | tf_op jit(solution)/shard_map/reduce_scatter | solution.py:65
  83.3 53.3 %copy-start.3 = (bf16[1024,1024]{0,1:T(8,128)(2,1)}, bf16[1024,1024]{0,1:T(8,128)(2,1)S(1)}, u32[]{:S(2)}) copy-start(bf16[1024,1024]{0,1:T(8,128)(2,1)S(1)} %copy.35) | copy-start | bytes 6291460
  132.7 5.4 %slice-start = ((s8[8388608]{0:T(1024)(128)(4,1)}), s8[4194304]{0:T(1024)(128)(4,1)S(1)}, s32[]{:S(2)}) async-start(s8[8388608]{0:T(1024)(128)(4,1)} %bitcast.63), calls=%async_computation.7 | async-start | bytes 8388608
  135.6 2.5 copy-start
  135.6 3.7 %slice-start.1 = ((s8[8388608]{0:T(1024)(128)(4,1)}), s8[4194304]{0:T(1024)(128)(4,1)S(1)}, s32[]{:S(2)}) async-start(s8[8388608]{0:T(1024)(128)(4,1)} %bitcast.63), calls=%async_computation.8 | async-start | bytes 8388608
  139.3 3.0 %copy-start.2 = (bf16[1024,1024]{0,1:T(8,128)(2,1)S(1)}, bf16[1024,1024]{0,1:T(8,128)(2,1)}, u32[]{:S(2)}) copy-start(bf16[1024,1024]{0,1:T(8,128)(2,1)} %all-gather.7.cloned.1.call-done) | copy-start | bytes 6291460
  142.3 67.4 %copy-start.5 = (bf16[128,1024]{1,0:T(8,128)(2,1)S(1)}, bf16[128,1024]{1,0:T(8,128)(2,1)}, u32[]{:S(2)}) copy-start(bf16[128,1024]{1,0:T(8,128)(2,1)} %param.7) | copy-start | bytes 786436
  209.7 29.1 %copy-start.1 = (bf16[1024,1024]{0,1:T(8,128)(2,1)S(1)}, bf16[1024,1024]{0,1:T(8,128)(2,1)}, u32[]{:S(2)}) copy-start(bf16[1024,1024]{0,1:T(8,128)(2,1)} %all-gather.13.cloned.1.call-done) | copy-start | bytes 6291460
  209.7 29.1 %copy-start.6 = (bf16[128,1024]{1,0:T(8,128)(2,1)S(1)}, bf16[128,1024]{1,0:T(8,128)(2,1)}, u32[]{:S(2)}) copy-start(bf16[128,1024]{1,0:T(8,128)(2,1)} %param.8) | copy-start | bytes 786436
Sparse Core Ops, SparseCore 0:
  9.6 19.4 all-gather.10
  31.1 49.2 all-gather.8
  83.1 49.5 all-gather.6
  135.2 49.6 all-gather.12
  187.4 47.4 all-gather.14
  237.3 29.9 reduce-scatter.1
where the time goes:
time: 276 us
  waiting for transfers between devices  127 us (46%)
  blocking collectives  81.9 us (30%)
  matrix products  33.7 us (12%)
  local copies, waits for them, and re-layouts  15.3 us (6%)
  between operations  14.3 us (5%)
  other arithmetic  3.43 us (1%)
    all_gather x1, waiting for transfers between devices, on_device(): lax.all_gather(keys, 'ctx', axis=0, tiled=True)  49.3 us
    all_gather x1, blocking collectives, on_device(): lax.all_gather(lse.T, 'ctx', axis=0, tiled=True)  30.9 us
    all_gather x1, blocking collectives, on_device(): lax.all_gather(delta.T, 'ctx', axis=0, tiled=True)  30.6 us
    all_gather x1, waiting for transfers between devices, on_device(): lax.all_gather(values, 'ctx', axis=0, tiled=True)  22.2 us
    all_gather x1, waiting for transfers between devices, on_device(): piece_d = lax.all_gather(d_attn, 'ctx', axis=0, tiled=True)  20.7 us
    all_gather x1, blocking collectives, on_device(): lax.all_gather(episode, 'ctx', axis=0, tiled=True)  20.4 us
    reduce_scatter x1, waiting for transfers between devices, on_device(): lax.psum_scatter(jnp.dot(attn, out_weight, preferred_element_type=jnp.flo...  16.7 us
    all_gather x1, waiting for transfers between devices, on_device(): lax.all_gather(d_out, 'head', axis=0, tiled=True)  16.6 us
  transfers between devices with their start and end apart: 6, of which 5 were waited for; matrix products, arithmetic and copies ran while one was open for 18% of the time, Pallas kernels for 0%

commit v1 on v0

--- a/solution.py
+++ b/solution.py
@@ -114,6 +114,83 @@
     return (mixed, d_queries, d_keys, d_values)
 
 
+def by_head(array, heads):
+    rows_local = array.shape[0]
+    return array.reshape(rows_local, heads, HD).transpose(1, 0, 2)
+
+
+def on_device_heads(queries, keys, values, episode, out_weight, d_out):
+    rows_local, width = queries.shape
+    heads = width // HD
+    scale = HD ** (-0.5)
+    ctx_count = lax.axis_size("ctx")
+    head_count = lax.axis_size("head")
+    own = heads // ctx_count
+    total = rows_local * ctx_count
+    window = 2 * ctx_count
+
+    def spread(arrays):
+        parts = [by_head(a, heads).reshape(ctx_count, own, rows_local, HD) for a in arrays]
+        got = lax.all_to_all(jnp.stack(parts, 1), "ctx", 0, 0, tiled=True)
+        return [got[:, i].transpose(1, 0, 2, 3).reshape(own, total, HD) for i in range(len(arrays))]
+
+    def collect(arrays):
+        parts = [a.reshape(own, ctx_count, rows_local, HD).transpose(1, 0, 2, 3) for a in arrays]
+        got = lax.all_to_all(jnp.stack(parts, 1), "ctx", 0, 0, tiled=True)
+        return [
+            got[:, i].reshape(heads, rows_local, HD).transpose(1, 0, 2).reshape(rows_local, width)
+            for i in range(len(arrays))
+        ]
+
+    d_all = lax.all_gather(d_out, "head", axis=0, tiled=True)
+    episode_all = lax.all_gather(episode, "ctx", axis=0, tiled=True)
+    q, k, v = spread([queries, keys, values])
+    d_attn = lax.dot_general(
+        d_all, out_weight, (((1,), (1,)), ((), ())), preferred_element_type=jnp.float32
+    ).astype(jnp.bfloat16)
+    (da,) = spread([d_attn])
+
+    time = time_steps(jnp.arange(total, dtype=jnp.int32), rows_local, ctx_count)
+    visible = (time[None, :] <= time[:, None]) & (
+        episode_all[:, None] - episode_all[None, :] < window
+    )
+    scores = jnp.einsum("hqd,hkd->hqk", q, k, preferred_element_type=jnp.float32) * scale
+    scores = jnp.where(visible[None], scores, floor_score)
+    top = jnp.max(scores, axis=2)
+    lse = top + jnp.log(jnp.sum(jnp.exp(scores - top[:, :, None]), axis=2))
+    probs = jnp.exp(scores - lse[:, :, None])
+    probs_low = probs.astype(jnp.bfloat16)
+    attn = jnp.einsum("hqk,hkd->hqd", probs_low, v, preferred_element_type=jnp.float32).astype(
+        jnp.bfloat16
+    )
+    (attn_rows,) = collect([attn])
+    delta = jnp.sum(da.astype(jnp.float32) * attn.astype(jnp.float32), axis=2)
+    d_probs = jnp.einsum("hqd,hkd->hqk", da, v, preferred_element_type=jnp.float32)
+    d_scores = (probs * (d_probs - delta[:, :, None])).astype(jnp.bfloat16)
+    dq = jnp.einsum("hqk,hkd->hqd", d_scores, k, preferred_element_type=jnp.float32)
+    dk = jnp.einsum("hqk,hqd->hkd", d_scores, q, preferred_element_type=jnp.float32)
+    dv = jnp.einsum("hqk,hqd->hkd", probs_low, da, preferred_element_type=jnp.float32)
+    d_queries, d_keys, d_values = collect(
+        [
+            (scale * dq).astype(jnp.bfloat16),
+            (scale * dk).astype(jnp.bfloat16),
+            dv.astype(jnp.bfloat16),
+        ]
+    )
+    share = jnp.dot(attn_rows, out_weight, preferred_element_type=jnp.float32).astype(jnp.bfloat16)
+    share = share.reshape(head_count, rows_local // head_count, share.shape[1])
+    shares = lax.all_to_all(share, "head", 0, 0, tiled=True)
+    mixed = jnp.sum(shares.astype(jnp.float32), axis=0).astype(jnp.bfloat16)
+    return (mixed, d_queries, d_keys, d_values)
+
+
+def route(queries, keys, values, episode, out_weight, d_out):
+    heads = queries.shape[1] // HD
+    if heads % lax.axis_size("ctx") == 0:
+        return on_device_heads(queries, keys, values, episode, out_weight, d_out)
+    return on_device(queries, keys, values, episode, out_weight, d_out)
+
+
 def solution(mesh):
     placed = (
         P("ctx", "head"),
@@ -124,7 +201,7 @@
         P(("ctx", "head"), None),
     )
     return jax.shard_map(
-        on_device,
+        route,
         mesh=mesh,
         in_specs=placed,
         out_specs=(P(("ctx", "head"), None), P("ctx", "head"), P("ctx", "head"), P("ctx", "head")),

time: 276 us -> 143 us (0.52)
  waiting for transfers between devices: 127 us -> 40.6 us
  blocking collectives: 81.9 us -> 26.5 us
  starting transfers between devices: 0.24 us -> 22.4 us
  matrix products: 33.7 us -> 24.4 us
  local copies, waits for them, and re-layouts: 15.3 us -> 9.72 us
    all_gather x5 -> x1, waiting for transfers between devices: 109 us -> 0.01 us  [on_device_heads(): d_all = lax.all_gather(d_out, 'head', axis=0, tiled=True)]
    all_gather x3 -> x1, blocking collectives: 81.9 us -> 26.5 us  [on_device_heads(): episode_all = lax.all_gather(episode, 'ctx', axis=0, tiled=True)]
    all_to_all x0 -> x5, waiting for transfers between devices: none -> 39.9 us  [the longest x2 24.4 us: collect(): got = lax.all_to_all(jnp.stack(parts, 1), 'ctx', 0, 0, tiled=True)]
    all_to_all x0 -> x5, starting transfers between devices: none -> 22.3 us  [the longest x2 11.9 us: spread(): got = lax.all_to_all(jnp.stack(parts, 1), 'ctx', 0, 0, tiled=True)]
    reduce_scatter x1 -> x0, waiting for transfers between devices: 16.7 us -> none  [on_device(): lax.psum_scatter(jnp.dot(attn, out_weight, preferred_element_type=jnp.flo...]
    dot_general x8, matrix products: 33.7 us -> 24.4 us  [the longest x1 6.63 us: on_device_heads(): lax.dot_general(d_all, out_weight, (((1,), (1,)), ((), ())), preferred_el...]
    reshape x1, local copies, waits for them, and re-layouts: 3.96 us -> 0.75 us  [by_head(): return array.reshape(rows_local, heads, HD).transpose(1, 0, 2)]
    all_gather x1 -> x0, local copies, waits for them, and re-layouts: 2.85 us -> none  [on_device(): lax.all_gather(values, 'ctx', axis=0, tiled=True)]
  transfers between devices with their start and end apart: 6 -> 6, of which waited for: 5 -> 4; matrix products, arithmetic and copies ran while one was open for 18% -> 10% of each run, Pallas kernels for 0% -> 0%
where the time goes in v1:
time: 143 us
  waiting for transfers between devices  40.6 us (28%)
  blocking collectives  26.5 us (19%)
  matrix products  24.4 us (17%)
  starting transfers between devices  22.4 us (16%)
  between operations  14.2 us (10%)
  local copies, waits for them, and re-layouts  9.72 us (7%)
  other arithmetic  4.78 us (3%)
    all_gather x1, blocking collectives, on_device_heads(): episode_all = lax.all_gather(episode, 'ctx', axis=0, tiled=True)  26.5 us
    all_to_all x2, waiting for transfers between devices, collect(): got = lax.all_to_all(jnp.stack(parts, 1), 'ctx', 0, 0, tiled=True)  24.4 us
    all_to_all x2, starting transfers between devices, spread(): got = lax.all_to_all(jnp.stack(parts, 1), 'ctx', 0, 0, tiled=True)  11.9 us
    all_to_all x1, waiting for transfers between devices, on_device_heads(): shares = lax.all_to_all(share, 'head', 0, 0, tiled=True)  10.1 us
    unnamed x22, local copies, waits for them, and re-layouts  7.03 us
    all_to_all x2, starting transfers between devices, collect(): got = lax.all_to_all(jnp.stack(parts, 1), 'ctx', 0, 0, tiled=True)  6.96 us
    dot_general x1, matrix products, on_device_heads(): lax.dot_general(d_all, out_weight, (((1,), (1,)), ((), ())), preferred_el...  6.63 us
    dot_general x1, matrix products, on_device_heads(): jnp.dot(attn_rows, out_weight, preferred_element_type=jnp.float32)  5.62 us
  transfers between devices with their start and end apart: 6, of which 4 were waited for; matrix products, arithmetic and copies ran while one was open for 10% of the time, Pallas kernels for 0%

profile of v1, /device:TPU:0, one launch (start us, length us, event | category | flops | bytes accessed | tf_op | source)
XLA Modules:
  0.0 142.6 jit_solution(13422726253963084531)
XLA Ops:
  7.2 1.1 copy.48
  8.3 1.1 copy.46
  9.4 1.1 copy.47
  10.7 1.0 copy.49
  11.6 7.3 %all-to-all-start = ((bf16[8,3,1,128,128]{3,4,2,1,0:T(8,128)(2,1)}), bf16[8,3,1,128,128]{3,4,2,1,0:T(8,128)(2,1)S(1)}, u32[]{:S(2)}, u32[]{:S(2)}) async-start(bf16[8,3,1,128,128]{3,4,2,1,0:T(8,128)(2,1)} %copy.49), calls=%async_computation | async-start | bytes 1572864 | tf_op jit(solution)/shard_map/all_to_all | solution.py:134
  19.6 26.5 %all-gather = s32[8,1,128]{2,1,0:T(1,128)S(1)} all-gather(s32[1,1,128]{2,1,0:T(1,128)S(1)} %bitcast.97), channel_id=1, replica_groups=mesh['ctx'=8,'head'=4] {'ctx'}, dimensions={0}, use_global_device_ids=true | all-gather | bytes 4608 | tf_op jit(solution)/shard_map/all_gather | solution.py:146
  46.8 2.7 %fusion.24 = (f32[1024]{0:T(1024)S(1)}, f32[1024,1024]{0,1:T(8,128)}) fusion(bf16[1024,128]{1,0:T(8,128)(2,1)S(1)} %bitcast.90, bf16[1024,128]{1,0:T(8,128)(2,1)S(1)} %bitcast.92, s32[1024]{0:T(1024)S(1)} %bitcast.96, s32[1024]{0:T(1024)S(1)} %fusion.16), kind=kOutput, calls=%fused_computation.42 | convolution fusion | flops 275774464 | bytes 4730880 | tf_op jit(solution)/shard_map/hqd,hkd->hqk/dot_general | solution.py:157
  49.5 6.6 %fusion.4 = bf16[16,8,8,128]{3,2,1,0:T(8,128)(2,1)S(1)} fusion(bf16[128,4096]{1,0:T(8,128)(2,1)} %all-gather.3.cloned.1.call-done, bf16[1024,4096]{1,0:T(8,128)(2,1)} %param.10), kind=kOutput, calls=%fused_computation.15 | convolution fusion | flops 1073872896 | bytes 9699328 | tf_op jit(solution)/shard_map/dot_general | solution.py:148
  56.9 4.6 %all-to-all-start.3 = ((bf16[8,1,1,128,128]{4,3,2,1,0:T(8,128)(2,1)}), bf16[8,1,1,128,128]{4,3,2,1,0:T(8,128)(2,1)S(1)}, u32[]{:S(2)}, u32[]{:S(2)}) async-start(bf16[8,1,1,128,128]{4,3,2,1,0:T(8,128)(2,1)} %bitcast.76), calls=%async_computation.3 | async-start | bytes 524288 | tf_op jit(solution)/shard_map/all_to_all | solution.py:134
  61.5 2.8 %exponential_reduce_fusion = f32[1024]{0:T(1024)S(1)} fusion(f32[1024,1024]{0,1:T(8,128)} %get-tuple-element.15, f32[1024]{0:T(1024)S(1)} %get-tuple-element.14), kind=kLoop, calls=%fused_computation.3 | loop fusion | flops 2096128 | bytes 4202496 | tf_op jit(solution)/shard_map/reduce_sum | solution.py:160
  64.3 5.4 %all-to-all-done.3 = bf16[8,1,1,128,128]{4,3,2,1,0:T(8,128)(2,1)S(1)} async-done(((bf16[8,1,1,128,128]{4,3,2,1,0:T(8,128)(2,1)}), bf16[8,1,1,128,128]{4,3,2,1,0:T(8,128)(2,1)S(1)}, u32[]{:S(2)}, u32[]{:S(2)}) %all-to-all-start.3) | async-done | bytes 262176 | tf_op jit(solution)/shard_map/all_to_all | solution.py:134
  69.7 3.1 %multiply_reduce_fusion = (f32[1024]{0:T(1024)S(1)}, bf16[1024,128]{1,0:T(8,128)(2,1)S(1)}) fusion(bf16[8,1,1,128,128]{4,3,2,1,0:T(8,128)(2,1)S(1)} %all-to-all-done.3, bf16[1024,128]{1,0:T(8,128)(2,1)S(1)} %bitcast.79, f32[1024,1024]{0,1:T(8,128)} %get-tuple-element.15, f32[1024]{0:T(1024)S(1)} %log_add_fusion), kind=kOutput, calls=%fused_computation.18 | convolution fusion | flops 271186944 | bytes 4988928 | tf_op jit(solution)/shard_map/hqk,hkd->hqd/dot_general | solution.py:163
  73.6 3.4 %all-to-all-start.1 = ((bf16[8,1,1,128,128]{3,4,2,1,0:T(8,128)(2,1)}), bf16[8,1,1,128,128]{3,4,2,1,0:T(8,128)(2,1)S(1)}, u32[]{:S(2)}, u32[]{:S(2)}) async-start(bf16[8,1,1,128,128]{3,4,2,1,0:T(8,128)(2,1)} %copy.53), calls=%async_computation.1 | async-start | bytes 524288 | tf_op jit(solution)/shard_map/all_to_all | solution.py:139
  77.1 3.1 %multiply_convert_fusion = bf16[1024,1024]{0,1:T(8,128)(2,1)S(1)} fusion(f32[1024,1024]{0,1:T(8,128)} %get-tuple-element.15, bf16[1024,128]{1,0:T(8,128)(2,1)S(1)} %bitcast.77, bf16[1024,128]{1,0:T(8,128)(2,1)S(1)} %bitcast.80, f32[1024]{0:T(1024)S(1)} %get-tuple-element.16, f32[1024]{0:T(1024)S(1)} %log_add_fusion), kind=kOutput, calls=%fused_computation.1 | convolution fusion | flops 272629760 | bytes 6823936 | tf_op jit(solution)/shard_map/hqd,hkd->hqk/dot_general | solution.py:168
  80.1 5.1 %all-to-all-done.1 = bf16[8,1,1,128,128]{3,4,2,1,0:T(8,128)(2,1)S(1)} async-done(((bf16[8,1,1,128,128]{3,4,2,1,0:T(8,128)(2,1)}), bf16[8,1,1,128,128]{3,4,2,1,0:T(8,128)(2,1)S(1)}, u32[]{:S(2)}, u32[]{:S(2)}) %all-to-all-start.1) | async-done | bytes 262176 | tf_op jit(solution)/shard_map/all_to_all | solution.py:139
  85.2 5.6 %convolution_convert_fusion = bf16[128,4096]{1,0:T(8,128)(2,1)} fusion(bf16[128,1024]{0,1:T(8,128)(2,1)S(1)} %bitcast.81, bf16[1024,4096]{1,0:T(8,128)(2,1)} %param.10), kind=kOutput, calls=%fused_computation | convolution fusion | flops 1074266112 | bytes 9699328 | tf_op jit(solution)/shard_map/dot_general | solution.py:180
  90.8 3.5 %all-to-all-start.2 = ((bf16[4,32,4096]{2,1,0:T(8,128)(2,1)}), bf16[4,32,4096]{2,1,0:T(8,128)(2,1)S(1)}, u32[]{:S(2)}, u32[]{:S(2)}) async-start(bf16[4,32,4096]{2,1,0:T(8,128)(2,1)} %bitcast.18), calls=%async_computation.2 | async-start | bytes 2097152 | tf_op jit(solution)/shard_map/all_to_all | solution.py:182
  94.4 1.9 %fusion.2 = bf16[1024,128]{1,0:T(8,128)(2,1)S(1)} fusion(bf16[1024,1024]{0,1:T(8,128)(2,1)S(1)} %multiply_convert_fusion, bf16[1024,128]{1,0:T(8,128)(2,1)} %bitcast.93), kind=kOutput, calls=%fused_computation.13 | convolution fusion | flops 268697600 | bytes 2621440 | tf_op jit(solution)/shard_map/hqk,hkd->hqd/dot_general | solution.py:170
  97.7 1.0 pad_maximum_fusion.1
  98.7 10.1 %all-to-all-done.2 = bf16[4,32,4096]{2,1,0:T(8,128)(2,1)S(1)} async-done(((bf16[4,32,4096]{2,1,0:T(8,128)(2,1)}), bf16[4,32,4096]{2,1,0:T(8,128)(2,1)S(1)}, u32[]{:S(2)}, u32[]{:S(2)}) %all-to-all-start.2) | async-done | bytes 1048608 | tf_op jit(solution)/shard_map/all_to_all | solution.py:182
  108.8 3.5 %all-to-all-start.4 = ((bf16[8,3,1,128,128]{4,3,2,1,0:T(8,128)(2,1)}), bf16[8,3,1,128,128]{4,3,2,1,0:T(8,128)(2,1)S(1)}, u32[]{:S(2)}, u32[]{:S(2)}) async-start(bf16[8,3,1,128,128]{4,3,2,1,0:T(8,128)(2,1)} %pad_maximum_fusion.1), calls=%async_computation.4 | async-start | bytes 1572864 | tf_op jit(solution)/shard_map/all_to_all | solution.py:139
  112.4 0.9 reduce_sum.31
  113.3 19.3 %all-to-all-done.4 = bf16[8,3,1,128,128]{4,3,2,1,0:T(8,128)(2,1)S(1)} async-done(((bf16[8,3,1,128,128]{4,3,2,1,0:T(8,128)(2,1)}), bf16[8,3,1,128,128]{4,3,2,1,0:T(8,128)(2,1)S(1)}, u32[]{:S(2)}, u32[]{:S(2)}) %all-to-all-start.4) | async-done | bytes 786464 | tf_op jit(solution)/shard_map/all_to_all | solution.py:139
  133.8 0.9 copy.63
  (31 shorter events, 6.8 us)
Async XLA Ops:
  7.2 12.4 %copy-start.4 = (s32[128]{0:T(128)S(1)}, s32[128]{0:T(128)}, u32[]{:S(2)}) copy-start(s32[128]{0:T(128)} %param.9) | copy-start | bytes 1540
  11.6 34.5 %all-to-all-start = ((bf16[8,3,1,128,128]{3,4,2,1,0:T(8,128)(2,1)}), bf16[8,3,1,128,128]{3,4,2,1,0:T(8,128)(2,1)S(1)}, u32[]{:S(2)}, u32[]{:S(2)}) async-start(bf16[8,3,1,128,128]{3,4,2,1,0:T(8,128)(2,1)} %copy.49), calls=%async_computation | async-start | bytes 1572864 | tf_op jit(solution)/shard_map/all_to_all | solution.py:134
  18.9 30.6 %all-gather.3.cloned.1.call-start = ((), (), s32[]{:S(2)}) async-start(), calls=%async_computation.5 | async-start | bytes 1310720 | tf_op jit(solution)/shard_map/all_gather | solution.py:145
  46.4 3.1 %copy-start.1 = (bf16[8,1,1,128,128]{4,3,0,2,1:T(8,128)(2,1)}, bf16[8,1,1,128,128]{4,3,0,2,1:T(8,128)(2,1)S(1)}, u32[]{:S(2)}) copy-start(bf16[8,1,1,128,128]{4,3,0,2,1:T(8,128)(2,1)S(1)} %copy.66) | copy-start | bytes 786436
  46.6 26.2 %copy-start.3 = (bf16[8,1,1,128,128]{4,3,0,2,1:T(8,128)(2,1)}, bf16[8,1,1,128,128]{4,3,0,2,1:T(8,128)(2,1)S(1)}, u32[]{:S(2)}) copy-start(bf16[8,1,1,128,128]{4,3,0,2,1:T(8,128)(2,1)S(1)} %copy.67) | copy-start | bytes 786436
  56.9 12.8 %all-to-all-start.3 = ((bf16[8,1,1,128,128]{4,3,2,1,0:T(8,128)(2,1)}), bf16[8,1,1,128,128]{4,3,2,1,0:T(8,128)(2,1)S(1)}, u32[]{:S(2)}, u32[]{:S(2)}) async-start(bf16[8,1,1,128,128]{4,3,2,1,0:T(8,128)(2,1)} %bitcast.76), calls=%async_computation.3 | async-start | bytes 524288 | tf_op jit(solution)/shard_map/all_to_all | solution.py:134
  73.6 11.6 %all-to-all-start.1 = ((bf16[8,1,1,128,128]{3,4,2,1,0:T(8,128)(2,1)}), bf16[8,1,1,128,128]{3,4,2,1,0:T(8,128)(2,1)S(1)}, u32[]{:S(2)}, u32[]{:S(2)}) async-start(bf16[8,1,1,128,128]{3,4,2,1,0:T(8,128)(2,1)} %copy.53), calls=%async_computation.1 | async-start | bytes 524288 | tf_op jit(solution)/shard_map/all_to_all | solution.py:139
  90.8 18.0 %all-to-all-start.2 = ((bf16[4,32,4096]{2,1,0:T(8,128)(2,1)}), bf16[4,32,4096]{2,1,0:T(8,128)(2,1)S(1)}, u32[]{:S(2)}, u32[]{:S(2)}) async-start(bf16[4,32,4096]{2,1,0:T(8,128)(2,1)} %bitcast.18), calls=%async_computation.2 | async-start | bytes 2097152 | tf_op jit(solution)/shard_map/all_to_all | solution.py:182
  94.4 1.9 %copy-start.2 = (bf16[8,1,1,128,128]{4,3,0,2,1:T(8,128)(2,1)S(1)}, bf16[8,1,1,128,128]{4,3,0,2,1:T(8,128)(2,1)}, u32[]{:S(2)}) copy-start(bf16[8,1,1,128,128]{4,3,0,2,1:T(8,128)(2,1)} %copy-done.1) | copy-start | bytes 786436
  94.4 2.6 %copy-start = (f32[1024,1024]{0,1:T(8,128)S(1)}, f32[1024,1024]{0,1:T(8,128)}, u32[]{:S(2)}) copy-start(f32[1024,1024]{0,1:T(8,128)} %get-tuple-element.15) | copy-start | bytes 12582916
  108.8 23.8 %all-to-all-start.4 = ((bf16[8,3,1,128,128]{4,3,2,1,0:T(8,128)(2,1)}), bf16[8,3,1,128,128]{4,3,2,1,0:T(8,128)(2,1)S(1)}, u32[]{:S(2)}, u32[]{:S(2)}) async-start(bf16[8,3,1,128,128]{4,3,2,1,0:T(8,128)(2,1)} %pad_maximum_fusion.1), calls=%async_computation.4 | async-start | bytes 1572864 | tf_op jit(solution)/shard_map/all_to_all | solution.py:139
Sparse Core Ops, SparseCore 0:
  21.3 18.1 all-gather.2
